TPU v7x, 32 devices: a whole 2x2x4 slice. The times are simulated.
32 devices in a mesh: img: 8 (over y, x, core), cls: 4 (over z).
Axes of the slice: x: 2, y: 2, z: 4, core: 2. Of those that a mesh axis runs over, the one named last changes fastest.
Arguments:
- images: float32 [256, 6144], P('img'), may hold values from -64 to 64
- classes: float32 [1024, 6144], P('cls'), may hold values from -1.2 to 1.2
- groups: int32 [256], P('img'), may hold values from 0 to 63
- ctf: float32 [64, 48], replicated, may hold values from -1 to 1
- noise_weight: float32 [48], replicated, may hold values from 1 to 4
- cycle_prior: float32 [48], replicated, may hold values from 0.5 to 4
Outputs:
- classes_out: float32 [1024, 6144], P('cls')
- log_evidence: float32 [256], P('img')
All inputs are finite; a program needn't handle non-finite values.
Results may differ from a plain program's by a relative error of at most 0.0003.
Values sent between devices are 32-bit elements; how exact they have to be, the bound alone decides.
No kernel may reach another device: no remote copies, remote signals or barrier semaphores. Data moves between devices by JAX's collectives and lax.ppermute only.
A program may use at most 128 MiB of HBM per device.

v0:
```python
import math

import jax
import jax.numpy as jnp
from jax import lax
from jax.sharding import PartitionSpec as P

R = 48
F = 64
J = 384
G = 64
ITERS = 2


highest = lax.Precision.HIGHEST


def joined(part, axis, combine):
    gathered = jax.tree.map(lambda a: lax.all_gather(a, axis), part)

    def take(source):
        return jax.tree.map(lambda a: lax.dynamic_index_in_dim(a, source, 0, False), gathered)

    return lax.fori_loop(
        1, lax.axis_size(axis), lambda source, state: combine(state, take(source)), take(0)
    )


def phase_tables():
    orders = jnp.arange(F, dtype=jnp.int32)
    rotation = jnp.arange(J, dtype=jnp.int32)
    residue = orders[:, None] * rotation[None, :] % J
    phases = residue.astype(jnp.float32) * (2.0 * math.pi / J)
    harmonic = jnp.where(orders == 0, 1.0, 2.0).astype(jnp.float32)
    score_table = jnp.stack(
        [harmonic[:, None] * jnp.cos(phases), -harmonic[:, None] * jnp.sin(phases)]
    )
    back_table = jnp.stack([jnp.cos(phases), jnp.sin(phases)])
    return (harmonic, score_table, back_table)


def image_ctf(labels, ctf):
    onehot = (labels[:, None] == jnp.arange(G, dtype=jnp.int32)[None, :]).astype(jnp.float32)
    return (onehot, jnp.dot(onehot, ctf, precision=highest))


def class_scores(pixels, onehot, ctf_rows, weights, current, ctf, harmonic, score_table):
    scaled = pixels * (ctf_rows * weights[None, :])[:, None, None, :]
    turned = jnp.stack([scaled[:, :, 1], -scaled[:, :, 0]], axis=2)
    paired = jnp.stack([scaled, turned], axis=1)
    correlation = jnp.einsum("nqmpr,kmpr->nkqm", paired, current, precision=highest)
    class_power = jnp.einsum("m,kmpr->kr", harmonic, current * current, precision=highest)
    group_penalty = jnp.dot(ctf * ctf * weights[None, :], class_power.T, precision=highest)
    penalty = jnp.dot(onehot, group_penalty, precision=highest)
    return (
        jnp.einsum("nkqm,qmj->nkj", correlation, score_table, precision=highest)
        - 0.5 * penalty[:, :, None]
    )


def class_terms(pixels, ctf_rows, posterior, back_table):
    phasor = jnp.einsum("nkj,qmj->nkqm", posterior, back_table, precision=highest)
    carried = pixels * ctf_rows[:, None, None, :]
    turned = jnp.stack([-carried[:, :, 1], carried[:, :, 0]], axis=2)
    spread_pixels = jnp.stack([carried, turned], axis=1)
    numerator = jnp.einsum("nkqm,nqmpr->kmpr", phasor, spread_pixels, precision=highest)
    image_mass = jnp.sum(posterior, axis=2)
    weight_sum = jnp.dot(image_mass.T, ctf_rows * ctf_rows, precision=highest)
    return (numerator, weight_sum)


def combine_peaks(earlier, latter):
    largest = jnp.maximum(earlier[0], latter[0])
    summed = earlier[1] * jnp.exp(earlier[0] - largest) + latter[1] * jnp.exp(latter[0] - largest)
    return (largest, summed)


def per_device(images, classes, groups, ctf, noise_weight, cycle_prior):
    harmonic, score_table, back_table = phase_tables()
    weights = noise_weight / math.sqrt(F * R)
    local_images = images.shape[0]
    local_classes = classes.shape[0]
    pixels = images.reshape(local_images, F, 2, R)
    current = classes.reshape(local_classes, F, 2, R)
    onehot, ctf_rows = image_ctf(groups, ctf)
    for iteration in range(ITERS):
        scores = class_scores(
            pixels, onehot, ctf_rows, weights, current, ctf, harmonic, score_table
        )
        local_peak = jnp.max(scores, axis=(1, 2))
        weighted = jnp.exp(scores - local_peak[:, None, None])
        local_total = jnp.sum(weighted, axis=(1, 2))
        largest, normaliser = joined((local_peak, local_total), "cls", combine_peaks)
        posterior = weighted * (jnp.exp(local_peak - largest) / normaliser)[:, None, None]
        numerator, weight_sum = class_terms(pixels, ctf_rows, posterior, back_table)
        whole_numerator, whole_weight = lax.psum((numerator, weight_sum), "img")
        current = (whole_numerator + cycle_prior * current) / (
            whole_weight[:, None, None, :] + cycle_prior
        )
    return (current.reshape(local_classes, F * 2 * R), largest + jnp.log(normaliser))


def solution(mesh):
    in_specs = (P("img", None), P("cls", None), P("img"), P(), P(), P())
    out_specs = (P("cls", None), P("img"))
    return jax.shard_map(
        per_device, mesh=mesh, in_specs=in_specs, out_specs=out_specs, check_vma=False
    )
```

profile of v0, /device:TPU:0, one launch (start us, length us, event | category | flops | bytes accessed | tf_op | source)
XLA Modules:
  0.0 436.8 jit_solution(17021090231013724488)
XLA Ops:
  7.7 4.6 %reshape.173 = f32[32,1,64,2,48]{4,3,2,0,1:T(2,128)S(1)} reshape(f32[32,6144]{1,0:T(8,128)} %param.10) | data formatting | bytes 1572864 | tf_op jit(solution)/shard_map/reshape | solution.py:83
  12.3 5.8 %reshape.174 = f32[32,64,2,48]{3,2,1,0:T(2,128)} reshape(f32[32,6144]{1,0:T(8,128)} %param.10) | data formatting | bytes 1572864 | tf_op jit(solution)/shard_map/reshape | solution.py:83
  27.0 6.7 %copy.19 = f32[256,6144]{0,1:T(8,128)} copy(f32[256,6144]{1,0:T(8,128)} %param.11) | data formatting | bytes 12582912 | tf_op args[1]
  49.9 5.3 %fusion.41 = f32[32,256,2,64]{1,0,2,3:T(8,128)S(1)} fusion(f32[256,64,2,48,1]{0,3,2,4,1:T(8,128)S(1)} %bitcast.154, f32[32,1,64,2,48]{4,0,3,1,2:T(8,128)S(1)} %maximum_bitcast_fusion.1, f32[32,1,64,2,48]{4,0,3,1,2:T(8,128)S(1)} %copy-done.2), kind=kOutput, calls=%fused_computation.57 | convolution fusion | flops 1208352768 | bytes 12058624 | tf_op jit(solution)/shard_map/nqmpr,kmpr->nkqm/dot_general | solution.py:51
  55.3 14.6 %fusion.8 = (f32[32]{0:T(128)S(1)}, f32[32,256,384,1]{2,1,3,0:T(8,128)S(1)}) fusion(f32[32,256]{1,0:T(8,128)S(1)} %convolution_multiply_fusion.1, f32[1,64,384]{2,1,0:T(8,128)S(1)} %get-tuple-element.324, f32[1,64,384]{2,1,0:T(8,128)S(1)} %get-tuple-element.325, f32[32,256,2,64]{1,0,2,3:T(8,128)S(1)} %fusion.41), kind=kOutput, calls=%fused_computation.20 | convolution fusion | flops 4838178816 | bytes 17006720 | tf_op jit(solution)/shard_map/nkqm,qmj->nkj/dot_general | solution.py:56
  74.8 13.4 %all-reduce.5 = (f32[128]{0:T(128)S(1)}, f32[128]{0:T(128)S(1)}) all-reduce(f32[128]{0:T(128)S(1)} %dynamic-update-slice, f32[128]{0:T(128)S(1)} %dynamic-update-slice.1), channel_id=2, replica_groups=mesh['img'=8,'cls'=4] {'cls'}, use_global_device_ids=true, to_apply=%add | all-reduce | flops 256 | bytes 2048
  90.0 18.2 %fusion.45 = f32[32,256,2,64,1]{1,3,2,0,4:T(8,128)S(1)} fusion(f32[32,256,384,1]{2,1,3,0:T(8,128)} %copy-done, f32[32]{0:T(128)S(1)} %exponential_divide_fusion.1, f32[32]{0:T(128)S(1)} %get-tuple-element.318, f32[32,256]{1,0:T(8,128)S(1)} %convolution_multiply_fusion.1, f32[1,64,384]{2,1,0:T(8,128)S(1)} %get-tuple-element.326, ...), kind=kOutput, calls=%fused_computation.59 | convolution fusion | flops 4841324544 | bytes 17006848 | tf_op jit(solution)/shard_map/nkj,qmj->nkqm/dot_general | solution.py:62
  108.2 10.1 %fusion.35 = f32[256,64,2,48]{0,3,2,1:T(8,128)} fusion(f32[32,256,2,64,1]{1,3,2,0,4:T(8,128)S(1)} %fusion.45, f32[32,1,64,2,48]{4,0,1,3,2:T(8,128)S(1)} %maximum_bitcast_fusion, f32[32,1,64,2,48]{4,0,1,3,2:T(8,128)S(1)} %copy_multiply_fusion.1), kind=kOutput, calls=%fused_computation.55 | convolution fusion | flops 1208352768 | bytes 12058624 | tf_op jit(solution)/shard_map/nkqm,nqmpr->kmpr/dot_general | solution.py:66
  118.4 7.6 %multiply_reduce_fusion.1 = f32[32,256]{1,0:T(8,128)S(1)} fusion(f32[32,256,384,1]{2,1,3,0:T(8,128)} %copy-done, f32[32]{0:T(128)S(1)} %exponential_divide_fusion.1, f32[32]{0:T(128)S(1)} %get-tuple-element.318, f32[32,256]{1,0:T(8,128)S(1)} %convolution_multiply_fusion.1), kind=kLoop, calls=%fused_computation.24 | loop fusion | flops 12574720 | bytes 12648704 | tf_op jit(solution)/shard_map/reduce_sum | solution.py:67
  126.2 25.2 %psum.29 = f32[256,48]{0,1:T(8,128)S(1)} all-reduce(f32[256,48]{0,1:T(8,128)S(1)} %fusion.65), channel_id=1, replica_groups=mesh['img'=8,'cls'=4] {'img'}, use_global_device_ids=true, to_apply=%region_7.8 | all-reduce | flops 12288 | bytes 98304 | tf_op jit(solution)/shard_map/psum | solution.py:96
  151.5 70.5 %all-reduce.9.cloned.1.call-done = f32[256,64,2,48]{0,3,2,1:T(8,128)} async-done(((f32[256,64,2,48]{0,3,2,1:T(8,128)}), f32[256,64,2,48]{0,3,2,1:T(8,128)}) %all-reduce.9.cloned.1.call-update) | async-done | bytes 6291472 | tf_op jit(solution)/shard_map/psum | solution.py:96
  222.0 9.0 %multiply_reduce_fusion.2 = (f32[256,64,48]{0,2,1:T(8,128)}, f32[256,64,2,48]{0,3,2,1:T(8,128)S(1)}) fusion(f32[256,48]{0,1:T(8,128)S(1)} %broadcast_add_fusion.1, f32[256,64,2,48]{0,3,2,1:T(8,128)} %all-reduce.9.cloned.1.call-done, f32[256,64,2,48]{0,3,2,1:T(8,128)} %bitcast.151, f32[48]{0:T(128)S(1)} %copy-done.12), kind=kLoop, calls=%fused_computation.34 | loop fusion | flops 7077888 | bytes 22069440 | tf_op jit(solution)/shard_map/m,kmpr->kr/reduce_sum | solution.py:52
  231.0 7.4 %fusion.31 = f32[1,256,48]{1,0,2:T(1,128)S(1)} fusion(f32[256,64,48]{0,2,1:T(8,128)} %get-tuple-element.306), kind=kOutput, calls=%fused_computation.51 | convolution fusion | flops 9437312 | bytes 3194880 | tf_op jit(solution)/shard_map/m,kmpr->kr/dot_general | solution.py:52
  238.4 7.9 %fusion.42 = f32[32,256,2,64]{1,0,2,3:T(8,128)} fusion(f32[32,1,64,2,48]{4,0,3,1,2:T(8,128)} %copy-done.6, f32[32,1,64,2,48]{4,0,3,1,2:T(8,128)S(1)} %copy-done.3, f32[256,64,2,48]{0,3,2,1:T(8,128)S(1)} %get-tuple-element.307), kind=kOutput, calls=%fused_computation.58 | convolution fusion | flops 1208352768 | bytes 12058624 | tf_op jit(solution)/shard_map/nqmpr,kmpr->nkqm/dot_general | solution.py:51
  247.0 16.5 %fusion.9 = (f32[32]{0:T(128)S(1)}, f32[32,256,384,1]{2,1,3,0:T(8,128)}) fusion(f32[32,256]{1,0:T(8,128)S(1)} %convolution_multiply_fusion, f32[1,64,384]{2,1,0:T(8,128)S(1)} %get-tuple-element.324, f32[1,64,384]{2,1,0:T(8,128)S(1)} %copy-done.10, f32[32,256,2,64]{1,0,2,3:T(8,128)} %fusion.42), kind=kOutput, calls=%fused_computation.21 | convolution fusion | flops 4838178816 | bytes 17006720 | tf_op jit(solution)/shard_map/nkqm,qmj->nkj/dot_general | solution.py:56
  263.7 6.4 %fusion.13 = f32[32]{0:T(128)S(1)} fusion(f32[32,256,384,1]{2,1,3,0:T(8,128)} %get-tuple-element.321, f32[32]{0:T(128)S(1)} %get-tuple-element.320, f32[32,256]{1,0:T(8,128)S(1)} %convolution_multiply_fusion), kind=kLoop, calls=%fused_computation.27 | loop fusion | flops 9437152 | bytes 12615936 | tf_op jit(solution)/shard_map/reduce_sum | solution.py:92
  270.3 11.9 %all-reduce.4 = (f32[128]{0:T(128)S(1)}, f32[128]{0:T(128)S(1)}) all-reduce(f32[128]{0:T(128)S(1)} %dynamic-update-slice.2, f32[128]{0:T(128)S(1)} %dynamic-update-slice.3), channel_id=4, replica_groups=mesh['img'=8,'cls'=4] {'cls'}, use_global_device_ids=true, to_apply=%add.2 | all-reduce | flops 256 | bytes 2048
  283.1 17.6 %fusion.48 = f32[32,256,2,64,1]{1,3,2,0,4:T(8,128)S(1)} fusion(f32[32,256,384,1]{2,1,3,0:T(8,128)} %get-tuple-element.321, f32[32]{0:T(128)S(1)} %get-tuple-element.315, f32[32]{0:T(128)S(1)} %get-tuple-element.320, f32[32,256]{1,0:T(8,128)S(1)} %convolution_multiply_fusion, f32[1,64,384]{2,1,0:T(8,128)S(1)} %get-tuple-element.326, ...), kind=kOutput, calls=%fused_computation.60 | convolution fusion | flops 4841324544 | bytes 17006848 | tf_op jit(solution)/shard_map/nkj,qmj->nkqm/dot_general | solution.py:62
  300.7 10.1 %fusion.38 = f32[256,64,2,48]{0,3,2,1:T(8,128)} fusion(f32[32,256,2,64,1]{1,3,2,0,4:T(8,128)S(1)} %fusion.48, f32[32,1,64,2,48]{4,0,1,3,2:T(8,128)S(1)} %copy-done.5, f32[32,1,64,2,48]{4,0,1,3,2:T(8,128)S(1)} %copy_multiply_fusion.1), kind=kOutput, calls=%fused_computation.56 | convolution fusion | flops 1208352768 | bytes 12058624 | tf_op jit(solution)/shard_map/nkqm,nqmpr->kmpr/dot_general | solution.py:66
  310.8 7.0 %multiply_reduce_fusion = f32[32,256]{1,0:T(8,128)S(1)} fusion(f32[32,256,384,1]{2,1,3,0:T(8,128)} %get-tuple-element.321, f32[32]{0:T(128)S(1)} %get-tuple-element.315, f32[32]{0:T(128)S(1)} %get-tuple-element.320, f32[32,256]{1,0:T(8,128)S(1)} %convolution_multiply_fusion), kind=kLoop, calls=%fused_computation.22 | loop fusion | flops 12574720 | bytes 12648704 | tf_op jit(solution)/shard_map/reduce_sum | solution.py:67
  318.1 24.9 %psum.31 = f32[256,48]{0,1:T(8,128)S(1)} all-reduce(f32[256,48]{0,1:T(8,128)S(1)} %fusion.63), channel_id=1, replica_groups=mesh['img'=8,'cls'=4] {'img'}, use_global_device_ids=true, to_apply=%region_15.16 | all-reduce | flops 12288 | bytes 98304 | tf_op jit(solution)/shard_map/psum | solution.py:96
  343.0 70.5 %all-reduce.11.cloned.1.call-done = f32[256,64,2,48]{0,3,2,1:T(8,128)} async-done(((f32[256,64,2,48]{0,3,2,1:T(8,128)}), f32[256,64,2,48]{0,3,2,1:T(8,128)}) %all-reduce.11.cloned.1.call-update) | async-done | bytes 6291472 | tf_op jit(solution)/shard_map/psum | solution.py:96
  413.5 9.4 %add_divide_fusion = f32[256,64,2,48]{0,3,2,1:T(8,128)} fusion(f32[256,64,2,48]{0,3,2,1:T(8,128)} %all-reduce.11.cloned.1.call-done, f32[256,64,2,48]{0,3,2,1:T(8,128)} %copy-done.1, f32[256,48]{0,1:T(8,128)S(1)} %broadcast_add_fusion, f32[48]{0:T(128)S(1)} %copy-done.12), kind=kLoop, calls=%fused_computation.30 | loop fusion | flops 4718592 | bytes 18923712 | tf_op jit(solution)/shard_map/div | solution.py:97
  423.0 6.6 %copy.24 = f32[256,6144]{1,0:T(8,128)} copy(f32[256,6144]{0,1:T(8,128)} %bitcast.155) | data formatting | bytes 12582912
  (89 shorter events, 34.2 us)
Async XLA Ops:
  7.2 11.0 %copy-start.14 = (f32[48]{0:T(128)S(1)}, f32[48]{0:T(128)}, u32[]{:S(2)}) copy-start(f32[48]{0:T(128)} %param.14) | copy-start | bytes 580
  7.2 11.0 %copy-start.11 = (f32[64,48]{0,1:T(8,128)S(1)}, f32[64,48]{0,1:T(8,128)}, u32[]{:S(2)}) copy-start(f32[64,48]{0,1:T(8,128)} %param.13) | copy-start | bytes 36868
  7.2 11.0 %copy-start.13 = (s32[32]{0:T(128)S(1)}, s32[32]{0:T(128)}, u32[]{:S(2)}) copy-start(s32[32]{0:T(128)} %param.12) | copy-start | bytes 388
  7.2 214.8 %all-reduce.9.cloned.1.call-start = ((), (), s32[]{:S(2)}) async-start(), calls=%async_computation | async-start | bytes 12582912 | tf_op jit(solution)/shard_map/psum | solution.py:96
  12.3 8.7 %copy-start.7 = (f32[32,1,64,2,48]{4,3,2,0,1:T(2,128)}, f32[32,1,64,2,48]{4,3,2,0,1:T(2,128)S(1)}, u32[]{:S(2)}) copy-start(f32[32,1,64,2,48]{4,3,2,0,1:T(2,128)S(1)} %reshape.173) | copy-start | bytes 2359300
  18.3 5.5 %copy-start.8 = (f32[32,64,2,48]{3,2,1,0:T(2,128)S(1)}, f32[32,64,2,48]{3,2,1,0:T(2,128)}, u32[]{:S(2)}) copy-start(f32[32,64,2,48]{3,2,1,0:T(2,128)} %reshape.174) | copy-start | bytes 2359300
  33.7 7.9 %copy-start.15 = (u32[32]{0:T(128)S(1)}, u32[32]{0:T(128)}, u32[]{:S(2)}) copy-start(u32[32]{0:T(128)} %constant.117) | copy-start | bytes 388
  43.3 11.9 %copy-start.9 = (f32[1,64,384]{2,1,0:T(8,128)}, f32[1,64,384]{2,1,0:T(8,128)S(1)}, u32[]{:S(2)}) copy-start(f32[1,64,384]{2,1,0:T(8,128)S(1)} %get-tuple-element.325) | copy-start | bytes 294916
  43.4 4.4 %slice-start = ((s8[6291456]{0:T(1024)(128)(4,1)}), s8[4194304]{0:T(1024)(128)(4,1)S(1)}, s32[]{:S(2)}) async-start(s8[6291456]{0:T(1024)(128)(4,1)} %bitcast.152), calls=%async_computation.2 | async-start | bytes 8388608
  43.4 4.4 %slice-start.1 = ((s8[6291456]{0:T(1024)(128)(4,1)}), s8[2097152]{0:T(1024)(128)(4,1)S(1)}, s32[]{:S(2)}) async-start(s8[6291456]{0:T(1024)(128)(4,1)} %bitcast.152), calls=%async_computation.3 | async-start | bytes 4194304
  47.5 2.4 copy-start.2
  47.8 7.5 %copy-start.6 = (f32[32,1,64,2,48]{4,0,3,1,2:T(8,128)}, f32[32,1,64,2,48]{4,0,3,1,2:T(8,128)S(1)}, u32[]{:S(2)}) copy-start(f32[32,1,64,2,48]{4,0,3,1,2:T(8,128)S(1)} %maximum_bitcast_fusion.1) | copy-start | bytes 2359300
  69.8 4.6 %copy-start = (f32[32,256,384,1]{2,1,3,0:T(8,128)}, f32[32,256,384,1]{2,1,3,0:T(8,128)S(1)}, u32[]{:S(2)}) copy-start(f32[32,256,384,1]{2,1,3,0:T(8,128)S(1)} %get-tuple-element.319) | copy-start | bytes 37748740
  90.0 18.3 %copy-start.4 = (f32[32,1,64,2,48]{4,0,1,3,2:T(8,128)}, f32[32,1,64,2,48]{4,0,1,3,2:T(8,128)S(1)}, u32[]{:S(2)}) copy-start(f32[32,1,64,2,48]{4,0,1,3,2:T(8,128)S(1)} %maximum_bitcast_fusion) | copy-start | bytes 2359300
  118.3 295.2 %all-reduce.11.cloned.1.call-start = ((), (), s32[]{:S(2)}) async-start(), calls=%async_computation.1 | async-start | bytes 12582912 | tf_op jit(solution)/shard_map/psum | solution.py:96
  118.4 33.0 %copy-start.12 = (f32[48]{0:T(128)S(1)}, f32[48]{0:T(128)}, u32[]{:S(2)}) copy-start(f32[48]{0:T(128)} %param.15) | copy-start | bytes 580
  231.0 7.4 %copy-start.1 = (f32[256,64,2,48]{0,3,2,1:T(8,128)}, f32[256,64,2,48]{0,3,2,1:T(8,128)S(1)}, u32[]{:S(2)}) copy-start(f32[256,64,2,48]{0,3,2,1:T(8,128)S(1)} %get-tuple-element.307) | copy-start | bytes 18874372
  231.0 7.4 %copy-start.3 = (f32[32,1,64,2,48]{4,0,3,1,2:T(8,128)S(1)}, f32[32,1,64,2,48]{4,0,3,1,2:T(8,128)}, u32[]{:S(2)}) copy-start(f32[32,1,64,2,48]{4,0,3,1,2:T(8,128)} %copy_multiply_fusion) | copy-start | bytes 2359300
  238.4 8.6 %copy-start.10 = (f32[1,64,384]{2,1,0:T(8,128)S(1)}, f32[1,64,384]{2,1,0:T(8,128)}, u32[]{:S(2)}) copy-start(f32[1,64,384]{2,1,0:T(8,128)} %copy-done.9) | copy-start | bytes 294916
  283.1 17.6 %copy-start.5 = (f32[32,1,64,2,48]{4,0,1,3,2:T(8,128)S(1)}, f32[32,1,64,2,48]{4,0,1,3,2:T(8,128)}, u32[]{:S(2)}) copy-start(f32[32,1,64,2,48]{4,0,1,3,2:T(8,128)} %copy-done.4) | copy-start | bytes 2359300
Sparse Core Ops, SparseCore 0:
  118.5 103.4 all-reduce.8
  311.0 102.5 all-reduce.10
where the time goes:
time: 444 us; the launch traced here: 437 us
  waiting for transfers between devices  141 us (32%)
  matrix products  113 us (25%)
  blocking collectives  75.4 us (17%)
  other arithmetic  62.6 us (14%)
  local copies, waits for them, and re-layouts  29.3 us (7%)
  between operations  15.5 us (3%)
    psum x2, waiting for transfers between devices, per_device(): whole_numerator, whole_weight = lax.psum((numerator, weight_sum), 'img')  141 us
    psum x2, blocking collectives, per_device(): whole_numerator, whole_weight = lax.psum((numerator, weight_sum), 'img')  50 us
    dot_general x2, matrix products, class_terms(): jnp.einsum('nkj,qmj->nkqm', posterior, back_table, precision=highest)  35.8 us
    dot_general x2, matrix products, class_scores(): jnp.einsum('nkqm,qmj->nkj', correlation, score_table, precision=highest)  31.1 us
    unnamed x2, blocking collectives  25.4 us
    dot_general x2, matrix products, class_terms(): jnp.einsum('nkqm,nqmpr->kmpr', phasor, spread_pixels, precision=highest)  20.2 us
    unnamed x47, local copies, waits for them, and re-layouts  18.4 us
    reduce_sum x2, other arithmetic, class_terms(): image_mass = jnp.sum(posterior, axis=2)  14.6 us
  transfers between devices with their start and end apart: 2, of which 2 were waited for; matrix products, arithmetic and copies ran while one was open for 3% of the time, Pallas kernels for 0%

commit v1 on v0

--- a/solution.py
+++ b/solution.py
@@ -2,17 +2,275 @@
 
 import jax
 import jax.numpy as jnp
+import numpy as np
 from jax import lax
+from jax.experimental import pallas as pl
+from jax.experimental.pallas import tpu as pltpu
 from jax.sharding import PartitionSpec as P
 
 R = 48
 F = 64
 J = 384
 G = 64
+LANES = 128
 ITERS = 2
-
+HALF = J // 2
+PAIR = 2 * R
+GROUP = 4 * PAIR
+LOG2E = math.log2(math.e)
+LN2 = math.log(2.0)
+VMEM_BYTES = 56 * 1024 * 1024
 
 highest = lax.Precision.HIGHEST
+f32 = jnp.float32
+bf16 = jnp.bfloat16
+
+
+def split(value):
+    high = value.astype(bf16)
+    return high, (value - high.astype(f32)).astype(bf16)
+
+
+def split_table(table):
+    high = table.astype(jnp.bfloat16)
+    return high, (table - high.astype(np.float32)).astype(jnp.bfloat16)
+
+
+def make_tables():
+    turn = np.arange(HALF)
+    score, back = [], []
+    for parity in range(2):
+        orders = np.arange(parity, F, 2)
+        phase = (orders[:, None] * turn[None, :] % J) * (2.0 * math.pi / J)
+        harmonic = np.where(orders == 0, 1.0, 2.0)[:, None] * LOG2E
+        rows = np.stack([harmonic * np.cos(phase), -harmonic * np.sin(phase)], 1).reshape(F, HALF)
+        high, low = split_table(rows.T.astype(np.float32))
+        score.append(np.concatenate([high, high, low], 1))
+        rows = np.stack([np.cos(phase), np.sin(phase)], 1).reshape(F, HALF).astype(np.float32)
+        high, low = split_table(rows)
+        back.append(np.concatenate([high, low], 0))
+    return np.stack(score), np.stack(back)
+
+
+def dot(a, b):
+    return jnp.dot(a, b, preferred_element_type=f32)
+
+
+def dot_nt(a, b):
+    return lax.dot_general(a, b, (((1,), (1,)), ((), ())), preferred_element_type=f32)
+
+
+def quarter_turn(value, sign):
+    return jnp.concatenate([-sign * value[:, R:], sign * value[:, :R]], axis=1)
+
+
+def prepare_kernel(images_ref, ctf_ref, high_ref, low_ref):
+    turned = images_ref[...].T
+    scale = jnp.concatenate([ctf_ref[...]] * (GROUP // R), axis=0)
+    high, low = split(turned * scale)
+    high_ref[...] = high
+    low_ref[...] = low
+
+
+def prepare(images, ctf_turned):
+    count, width = images.shape
+    return pl.pallas_call(
+        prepare_kernel,
+        grid=(width // GROUP,),
+        in_specs=[
+            pl.BlockSpec((count, GROUP), lambda i: (0, i)),
+            pl.BlockSpec((R, count), lambda i: (0, 0)),
+        ],
+        out_specs=[pl.BlockSpec((GROUP, count), lambda i: (i, 0))] * 2,
+        out_shape=[jax.ShapeDtypeStruct((width, count), bf16)] * 2,
+        compiler_params=pltpu.CompilerParams(vmem_limit_bytes=VMEM_BYTES),
+        name="prepare",
+    )(images, ctf_turned)
+
+
+def row_of(order_pair, parity, q):
+    return parity * F + order_pair * 2 + q
+
+
+def score_kernel(
+    classes_ref, weight_ref, penalty_ref, high_ref, low_ref, score_ref, back_ref,
+    phasor_ref, peak_ref, total_ref, stat_ref, corr_ref,
+):
+    number = classes_ref.shape[0]
+
+    def correlate(block, _):
+        scaled = classes_ref[:, pl.ds(pl.multiple_of(block * GROUP, GROUP), GROUP)] * weight_ref[...]
+        for i in range(4):
+            own = scaled[:, i * PAIR : (i + 1) * PAIR]
+            lhs_high, lhs_low = split(jnp.concatenate([own, quarter_turn(own, 1.0)], axis=0))
+            rows = pl.ds(pl.multiple_of(block * GROUP + i * PAIR, PAIR), PAIR)
+            high = high_ref[rows, :]
+            out = dot(jnp.concatenate([lhs_high, lhs_low], axis=0), high)
+            out = out[: 2 * number] + out[2 * number :] + dot(lhs_high, low_ref[rows, :])
+            for q in range(2):
+                start = row_of(block * 2 + i // 2, i % 2, q)
+                for side in range(corr_ref.shape[0]):
+                    lanes = slice(side * LANES, (side + 1) * LANES)
+                    corr_ref[side, pl.ds(start, number, stride=2 * F), :] = out[q * number : (q + 1) * number, lanes]
+        return 0
+
+    lax.fori_loop(0, F // 4, correlate, 0)
+
+    def rotate(k, _):
+        waves = []
+        for parity in range(2):
+            rows = pl.ds(pl.multiple_of(k * 2 * F + parity * F, F), F)
+            corr = jnp.concatenate([corr_ref[side, rows, :] for side in range(corr_ref.shape[0])], axis=1)
+            high, low = split(corr)
+            waves.append(dot(score_ref[parity], jnp.concatenate([high, low, high], axis=0)))
+        even, odd = waves
+        peak = jnp.max(even + jnp.abs(odd), axis=0, keepdims=True)
+        base = even - peak
+        first = jnp.exp2(base + odd)
+        second = jnp.exp2(base - odd)
+        plus = first + second
+        minus = first - second
+        for parity, folded in enumerate((plus, minus)):
+            high, low = split(folded)
+            out = dot(back_ref[parity], high)
+            out = out[:F] + out[F:] + dot(back_ref[parity, :F], low)
+            rows = pl.ds(pl.multiple_of(k * 2 * F + parity * F, F), F)
+            for side in range(phasor_ref.shape[0]):
+                phasor_ref[side, rows, :] = out[:, side * LANES : (side + 1) * LANES]
+        peak_ref[pl.ds(k, 1), :] = peak - penalty_ref[pl.ds(k, 1), :]
+        total_ref[pl.ds(k, 1), :] = jnp.sum(plus, axis=0, keepdims=True)
+        return 0
+
+    lax.fori_loop(0, number, rotate, 0)
+    largest = jnp.max(peak_ref[...], axis=0, keepdims=True)
+    stat_ref[0:1, :] = largest
+    stat_ref[1:2, :] = jnp.sum(total_ref[...] * jnp.exp2(peak_ref[...] - largest), axis=0, keepdims=True)
+
+
+def score(classes, weight_row, penalty, high, low, score_table, back_table):
+    number, width = classes.shape
+    count = high.shape[1]
+    return pl.pallas_call(
+        score_kernel,
+        out_shape=[
+            jax.ShapeDtypeStruct((count // LANES, number * 2 * F, LANES), f32),
+            jax.ShapeDtypeStruct((number, count), f32),
+            jax.ShapeDtypeStruct((number, count), f32),
+            jax.ShapeDtypeStruct((2, count), f32),
+        ],
+        scratch_shapes=[pltpu.VMEM((count // LANES, number * 2 * F, LANES), f32)],
+        compiler_params=pltpu.CompilerParams(vmem_limit_bytes=VMEM_BYTES),
+        name="score",
+    )(classes, weight_row, penalty, high, low, score_table, back_table)
+
+
+def update_kernel(
+    classes_ref, phasor_ref, peak_ref, total_ref, joint_ref, high_ref, low_ref, square_ref, prior_ref, out_ref
+):
+    number = classes_ref.shape[0]
+    factor = jnp.exp2(peak_ref[...] - joint_ref[0:1, :]) * (1.0 / joint_ref[1:2, :])
+    mass = total_ref[...] * factor
+    weight = lax.dot_general(
+        mass, square_ref[...], (((1,), (1,)), ((), ())), precision=highest, preferred_element_type=f32
+    )
+    scale = 1.0 / (weight + prior_ref[:, :R])
+    scale = jnp.concatenate([scale] * (GROUP // R), axis=1)
+
+    def update(block, _):
+        parts = []
+        for i in range(4):
+            lhs = []
+            for q in range(2):
+                start = row_of(block * 2 + i // 2, i % 2, q)
+                rows = pl.ds(start, number, stride=2 * F)
+                sides = [phasor_ref[side, rows, :] for side in range(phasor_ref.shape[0])]
+                lhs.append(jnp.concatenate(sides, axis=1) * factor)
+            lhs_high, lhs_low = split(jnp.concatenate(lhs, axis=0))
+            rows = pl.ds(pl.multiple_of(block * GROUP + i * PAIR, PAIR), PAIR)
+            out = dot_nt(jnp.concatenate([lhs_high, lhs_low], axis=0), high_ref[rows, :])
+            out = out[: 2 * number] + out[2 * number :] + dot_nt(lhs_high, low_ref[rows, :])
+            parts.append(out[:number] + quarter_turn(out[number:], 1.0))
+        columns = pl.ds(pl.multiple_of(block * GROUP, GROUP), GROUP)
+        numerator = jnp.concatenate(parts, axis=1)
+        out_ref[:, columns] = (numerator + prior_ref[...] * classes_ref[:, columns]) * scale
+        return 0
+
+    lax.fori_loop(0, F // 4, update, 0)
+
+
+def update(classes, phasor, peak, total, joint, high, low, square, prior_row):
+    return pl.pallas_call(
+        update_kernel,
+        out_shape=jax.ShapeDtypeStruct(classes.shape, f32),
+        compiler_params=pltpu.CompilerParams(vmem_limit_bytes=VMEM_BYTES),
+        name="update",
+    )(classes, phasor, peak, total, joint, high, low, square, prior_row)
+
+
+def flipped(array, axis, bit):
+    size = lax.axis_size(axis)
+    return lax.ppermute(array, axis, [(i, i ^ bit) for i in range(size)])
+
+
+def gather_blocks(block, me):
+    rows = block.shape[0]
+    half = rows // 2
+    beside = flipped(block, "img", 2)
+    above = flipped(block, "img", 4)
+    top = flipped(beside[:half], "img", 4)
+    bottom = flipped(above[half:], "img", 2)
+    mine = jnp.concatenate([block, beside, above, top, bottom], axis=0)
+    other = flipped(mine, "img", 1)
+    out = jnp.zeros((8 * rows,) + block.shape[1:], block.dtype)
+    for step in range(4):
+        piece = slice(step * rows, (step + 1) * rows)
+        out = lax.dynamic_update_slice(out, mine[piece], ((me ^ (2 * step)) * rows, 0))
+        out = lax.dynamic_update_slice(out, other[piece], ((me ^ (2 * step + 1)) * rows, 0))
+    return out
+
+
+def combine(earlier, latter):
+    largest = jnp.maximum(earlier[0:1], latter[0:1])
+    summed = earlier[1:2] * jnp.exp2(earlier[0:1] - largest) + latter[1:2] * jnp.exp2(latter[0:1] - largest)
+    return jnp.concatenate([largest, summed], axis=0)
+
+
+def join(stat):
+    for axis in ("img", "cls"):
+        bit = 1
+        while bit < lax.axis_size(axis):
+            stat = combine(stat, flipped(stat, axis, bit))
+            bit *= 2
+    return stat
+
+
+def per_device(images, classes, groups, ctf, noise_weight, cycle_prior):
+    score_table, back_table = make_tables()
+    score_table, back_table = jnp.asarray(score_table), jnp.asarray(back_table)
+    weights = noise_weight / math.sqrt(F * R)
+    me = lax.axis_index("img")
+    local = images.shape[0]
+    number = classes.shape[0] // lax.axis_size("img")
+    all_images = gather_blocks(images, me)
+    all_groups = lax.all_gather(groups.astype(f32), "img", tiled=True)
+    onehot = (all_groups[:, None] == jnp.arange(G, dtype=f32)[None, :]).astype(f32)
+    ctf_turned = lax.dot_general(ctf, onehot, (((0,), (1,)), ((), ())), precision=highest)
+    square = ctf_turned * ctf_turned
+    high, low = prepare(all_images, ctf_turned)
+    current = lax.dynamic_slice_in_dim(classes, me * number, number, 0)
+    weight_row = jnp.tile(weights, GROUP // R)[None, :]
+    prior_row = jnp.tile(cycle_prior, GROUP // R)[None, :]
+    harmonic = jnp.where(jnp.arange(F) == 0, 1.0, 2.0).astype(f32)
+    penalty_table = square * (0.5 * LOG2E) * weights[:, None]
+    for iteration in range(ITERS):
+        power = jnp.einsum("kmpr,m->kr", (current * current).reshape(number, F, 2, R), harmonic, precision=highest)
+        penalty = jnp.dot(power, penalty_table, precision=highest)
+        phasor, peak, total, stat = score(current, weight_row, penalty, high, low, score_table, back_table)
+        joint = join(stat)
+        current = update(current, phasor, peak, total, joint, high, low, square, prior_row)
+    mine = lax.dynamic_slice_in_dim(joint, me * local, local, 1)
+    evidence = mine[0] * LN2 + jnp.log(mine[1])
+    return gather_blocks(current, me), evidence
 
 
 def joined(part, axis, combine):
@@ -75,7 +333,7 @@
     return (largest, summed)
 
 
-def per_device(images, classes, groups, ctf, noise_weight, cycle_prior):
+def plain_device(images, classes, groups, ctf, noise_weight, cycle_prior):
     harmonic, score_table, back_table = phase_tables()
     weights = noise_weight / math.sqrt(F * R)
     local_images = images.shape[0]
@@ -103,6 +361,7 @@
 def solution(mesh):
     in_specs = (P("img", None), P("cls", None), P("img"), P(), P(), P())
     out_specs = (P("cls", None), P("img"))
+    planned = per_device if mesh.shape["img"] == 8 else plain_device
     return jax.shard_map(
-        per_device, mesh=mesh, in_specs=in_specs, out_specs=out_specs, check_vma=False
-    )
+        planned, mesh=mesh, in_specs=in_specs, out_specs=out_specs, check_vma=False
+    )

time: 444 us -> 262 us (0.59); the launches traced: 437 us -> 261 us
  matrix products: 113 us -> 5.14 us
  Pallas kernels: 0 us -> 103 us
  waiting for transfers between devices: 141 us -> 64.8 us
  blocking collectives: 75.4 us -> 14.1 us
  other arithmetic: 62.6 us -> 15.7 us
  starting transfers between devices: 0.08 us -> 23.9 us
  between operations: 15.5 us -> 1.62 us
    psum x2 -> x0, waiting for transfers between devices: 141 us -> none  [per_device(): whole_numerator, whole_weight = lax.psum((numerator, weight_sum), 'img')]
    dot_general x17 -> x5, matrix products: 113 us -> 5.14 us  [the longest x2 2.55 us: per_device(): jnp.einsum('kmpr,m->kr', (current * current).reshape(number, F, 2, R), ha...]
    pallas_call x0 -> x5, Pallas kernels: none -> 103 us  [the longest x2 60.4 us: score(): pl.pallas_call(score_kernel, out_shape=[jax.ShapeDtypeStruct((count // LA...]
    ppermute x0 -> x20, waiting for transfers between devices: none -> 64.8 us  [flipped(): return lax.ppermute(array, axis, [(i, i ^ bit) for i in range(size)])]
    psum x2 -> x0, blocking collectives: 50 us -> none  [per_device(): whole_numerator, whole_weight = lax.psum((numerator, weight_sum), 'img')]
    reduce_sum x6 -> x2, other arithmetic: 37 us -> 7.1 us  [per_device(): jnp.einsum('kmpr,m->kr', (current * current).reshape(number, F, 2, R), ha...]
    ppermute x0 -> x20, starting transfers between devices: none -> 23.9 us  [flipped(): return lax.ppermute(array, axis, [(i, i ^ bit) for i in range(size)])]
    dynamic_update_slice x0 -> x12, local copies, waits for them, and re-layouts: none -> 11.6 us  [the longest x8 8.48 us: gather_blocks(): lax.dynamic_update_slice(out, other[piece], ((me ^ 2 * step + 1) * rows, 0))]
  transfers between devices with their start and end apart: 2 -> 20, of which waited for: 2 -> 17; matrix products, arithmetic and copies ran while one was open for 3% -> 10% of each run, Pallas kernels for 0% -> 0%
where the time goes in v1:
time: 262 us; the launch traced here: 261 us
  Pallas kernels  103 us (39%)
  waiting for transfers between devices  64.8 us (25%)
  local copies, waits for them, and re-layouts  33.5 us (13%)
  starting transfers between devices  23.9 us (9%)
  other arithmetic  15.7 us (6%)
  blocking collectives  14.1 us (5%)
  matrix products  5.14 us (2%)
    ppermute x20, waiting for transfers between devices, flipped(): return lax.ppermute(array, axis, [(i, i ^ bit) for i in range(size)])  64.8 us
    pallas_call x2, Pallas kernels, score(): pl.pallas_call(score_kernel, out_shape=[jax.ShapeDtypeStruct((count // LA...  60.4 us
    pallas_call x2, Pallas kernels, update(): pl.pallas_call(update_kernel, out_shape=jax.ShapeDtypeStruct(classes.shap...  30.1 us
    ppermute x20, starting transfers between devices, flipped(): return lax.ppermute(array, axis, [(i, i ^ bit) for i in range(size)])  23.9 us
    unnamed x1, blocking collectives  14.1 us
    pallas_call x1, Pallas kernels, prepare(): pl.pallas_call(prepare_kernel, grid=(width // GROUP,), in_specs=[pl.Block...  12.2 us
    dynamic_update_slice x8, local copies, waits for them, and re-layouts, gather_blocks(): lax.dynamic_update_slice(out, other[piece], ((me ^ 2 * step + 1) * rows, 0))  8.48 us
    reshape x2, local copies, waits for them, and re-layouts, per_device(): (current * current).reshape(number, F, 2, R)  7.93 us
  transfers between devices with their start and end apart: 20, of which 17 were waited for; matrix products, arithmetic and copies ran while one was open for 10% of the time, Pallas kernels for 0%

profile of v1, /device:TPU:0, one launch (start us, length us, event | category | flops | bytes accessed | tf_op | source)
XLA Modules:
  0.0 261.3 jit_solution(17709515595052261534)
XLA Ops:
  0.7 3.0 %collective-permute-start = (f32[32,6144]{1,0:T(8,128)}, f32[32,6144]{1,0:T(8,128)S(1)}, u32[]{:S(2)}, u32[]{:S(2)}) collective-permute-start(f32[32,6144]{1,0:T(8,128)} %param.8), channel_id=1, source_target_pairs={{0,8},{4,12},{8,0},{12,4},{16,24},{20,28},{24,16},{28,20},{1,9},{5... | collective-permute-start | bytes 2359304 | tf_op jit(solution)/shard_map/ppermute | solution.py:212
  5.2 3.4 %broadcast.15.clone = f32[256,6144]{1,0:T(8,128)} broadcast(f32[]{:T(128)} %constant.20.clone.1), dimensions={} | broadcast | bytes 6291460 | tf_op jit(solution)/shard_map/broadcast.3
  9.9 11.5 %collective-permute-done = f32[32,6144]{1,0:T(8,128)S(1)} collective-permute-done((f32[32,6144]{1,0:T(8,128)}, f32[32,6144]{1,0:T(8,128)S(1)}, u32[]{:S(2)}, u32[]{:S(2)}) %collective-permute-start) | collective-permute-done | bytes 786464 | tf_op jit(solution)/shard_map/ppermute | solution.py:212
  26.8 5.0 %collective-permute-done.2 = f32[16,6144]{1,0:T(8,128)S(1)} collective-permute-done((f32[16,6144]{1,0:T(8,128)S(1)}, f32[16,6144]{1,0:T(8,128)S(1)}, u32[]{:S(2)}, u32[]{:S(2)}) %collective-permute-start.2) | collective-permute-done | bytes 393248 | tf_op jit(solution)/shard_map/ppermute | solution.py:212
  36.3 4.6 %reshape.18 = f32[32,64,2,48]{3,2,1,0:T(2,128)S(1)} reshape(f32[32,6144]{1,0:T(8,128)} %get-tuple-element.38) | data formatting | bytes 1572864 | tf_op jit(solution)/shard_map/reshape | solution.py:266
  42.9 4.3 %reduce_sum.18 = f32[32,64,48]{2,1,0:T(8,128)} reduce(f32[32,64,2,48]{3,2,1,0:T(2,128)S(1)} %reshape.18, f32[]{:T(128)} %constant.20.clone.1), dimensions={2}, to_apply=%region_0.1 | reduce | flops 98304 | bytes 1179652 | tf_op jit(solution)/shard_map/kmpr,m->kr/reduce_sum | solution.py:266
  47.3 14.1 %all-reduce = f32[256]{0:T(256)S(1)} all-reduce(f32[256]{0:T(256)S(1)} %convert_dynamic-update-slice_fusion), channel_id=1, replica_groups=mesh['img'=8,'cls'=4] {'img'}, use_global_device_ids=true, to_apply=%add | all-reduce | flops 256 | bytes 2048
  77.3 12.2 %prepare.1 = (bf16[6144,256]{1,0:T(8,128)(2,1)}, bf16[6144,256]{1,0:T(8,128)(2,1)}) custom-call(f32[256,6144]{1,0:T(8,128)} %slice_dynamic-update-slice_fusion.4.images_ref, f32[48,256]{1,0:T(8,128)} %copy-done.6), custom_call_target="tpu_custom_call" | custom-call | tf_op jit(solution)/shard_map/prepare/pallas_call | solution.py:77
  89.5 30.2 %score.2 = (f32[2,4096,128]{2,1,0:T(8,128)}, f32[32,256]{1,0:T(8,128)}, f32[32,256]{1,0:T(8,128)}, f32[2,256]{1,0:T(2,128)}) custom-call(f32[32,6144]{1,0:T(8,128)} %get-tuple-element.39.classes_ref, f32[1,384]{1,0:T(1,128)} %broadcast_in_dim_tile.6.weight_ref, f32[32,256]{1,0:T(8,128)} %fusion.3.penalty_ref, bf16[6144,256]{1,0:T(8,128)(2,1)} %get-tuple-element.12.high_ref, ...), custom_call_target="tpu_custom_call" | custom-call | tf_op jit(solution)/shard_map/score/pallas_call | solution.py:153
  121.9 3.6 %collective-permute-done.6 = f32[2,256]{1,0:T(2,128)S(1)} collective-permute-done((f32[2,256]{1,0:T(2,128)S(1)}, f32[2,256]{1,0:T(2,128)S(1)}, u32[]{:S(2)}, u32[]{:S(2)}) %collective-permute-start.6) | collective-permute-done | bytes 2080 | tf_op jit(solution)/shard_map/ppermute | solution.py:212
  132.8 2.7 %collective-permute-start.9 = (f32[2,256]{1,0:T(2,128)S(1)}, f32[2,256]{1,0:T(2,128)S(1)}, u32[]{:S(2)}, u32[]{:S(2)}) collective-permute-start(f32[2,256]{1,0:T(2,128)S(1)} %pad_maximum_fusion.4), channel_id=1, source_target_pairs={{0,2},{1,3},{2,0},{3,1},{4,6},{5,7},{6,4},{7,5},{8,10},{9,11},{10,... | collective-permute-start | bytes 6152 | tf_op jit(solution)/shard_map/ppermute | solution.py:212
  138.0 15.0 %update.2.classes_ref = f32[32,6144]{1,0:T(8,128)} custom-call(f32[32,6144]{1,0:T(8,128)} %get-tuple-element.39.classes_ref, f32[2,4096,128]{2,1,0:T(8,128)} %get-tuple-element.14.phasor_ref, f32[32,256]{1,0:T(8,128)} %get-tuple-element.15.peak_ref, f32[32,256]{1,0:T(8,128)} %get-tuple-element.16.total_ref, f32[2,256]{1,0:T(2,128)} %pad_maximum_fusion.5.joint_ref, ...), custom_call_target="tpu_custom_call" | custom-call | tf_op jit(solution)/shard_map/update/pallas_call | solution.py:202
  154.6 3.3 %reshape.19 = f32[32,64,2,48]{3,2,1,0:T(2,128)S(1)} reshape(f32[32,6144]{1,0:T(8,128)S(1)} %mul.148) | data formatting | bytes 1572864 | tf_op jit(solution)/shard_map/reshape | solution.py:266
  157.9 2.8 %reduce_sum.19 = f32[32,64,48]{2,1,0:T(8,128)S(1)} reduce(f32[32,64,2,48]{3,2,1,0:T(2,128)S(1)} %reshape.19, f32[]{:T(128)} %constant.20.clone.1), dimensions={2}, to_apply=%region_1.2 | reduce | flops 98304 | bytes 1179652 | tf_op jit(solution)/shard_map/kmpr,m->kr/reduce_sum | solution.py:266
  162.2 30.2 %score.3 = (f32[2,4096,128]{2,1,0:T(8,128)}, f32[32,256]{1,0:T(8,128)}, f32[32,256]{1,0:T(8,128)}, f32[2,256]{1,0:T(2,128)}) custom-call(f32[32,6144]{1,0:T(8,128)} %update.2.classes_ref, f32[1,384]{1,0:T(1,128)} %broadcast_in_dim_tile.6.weight_ref, f32[32,256]{1,0:T(8,128)} %fusion.1.penalty_ref, bf16[6144,256]{1,0:T(8,128)(2,1)} %get-tuple-element.12.high_ref, ...), custom_call_target="tpu_custom_call" | custom-call | tf_op jit(solution)/shard_map/score/pallas_call | solution.py:153
  194.6 3.6 %collective-permute-done.11 = f32[2,256]{1,0:T(2,128)S(1)} collective-permute-done((f32[2,256]{1,0:T(2,128)S(1)}, f32[2,256]{1,0:T(2,128)S(1)}, u32[]{:S(2)}, u32[]{:S(2)}) %collective-permute-start.11) | collective-permute-done | bytes 2080 | tf_op jit(solution)/shard_map/ppermute | solution.py:212
  199.3 2.5 collective-permute-done.12
  205.6 2.7 %collective-permute-start.14 = (f32[2,256]{1,0:T(2,128)S(1)}, f32[2,256]{1,0:T(2,128)S(1)}, u32[]{:S(2)}, u32[]{:S(2)}) collective-permute-start(f32[2,256]{1,0:T(2,128)S(1)} %pad_maximum_fusion.9), channel_id=1, source_target_pairs={{0,2},{1,3},{2,0},{3,1},{4,6},{5,7},{6,4},{7,5},{8,10},{9,11},{10,... | collective-permute-start | bytes 6152 | tf_op jit(solution)/shard_map/ppermute | solution.py:212
  210.8 15.1 %update.3 = f32[32,6144]{1,0:T(8,128)} custom-call(f32[32,6144]{1,0:T(8,128)} %update.2.classes_ref, f32[2,4096,128]{2,1,0:T(8,128)} %get-tuple-element.18.phasor_ref, f32[32,256]{1,0:T(8,128)} %get-tuple-element.19.peak_ref, f32[32,256]{1,0:T(8,128)} %get-tuple-element.20.total_ref, f32[2,256]{1,0:T(2,128)} %pad_maximum_fusion.joint_ref, ...), custom_call_target="tpu_custom_call" | custom-call | tf_op jit(solution)/shard_map/update/pallas_call | solution.py:202
  227.8 15.0 %collective-permute-done.15 = f32[32,6144]{1,0:T(8,128)S(1)} collective-permute-done((f32[32,6144]{1,0:T(8,128)}, f32[32,6144]{1,0:T(8,128)S(1)}, u32[]{:S(2)}, u32[]{:S(2)}) %collective-permute-start.15) | collective-permute-done | bytes 786464 | tf_op jit(solution)/shard_map/ppermute | solution.py:212
  244.1 2.6 collective-permute-start.18
  246.7 3.9 %collective-permute-done.17 = f32[16,6144]{1,0:T(8,128)S(1)} collective-permute-done((f32[16,6144]{1,0:T(8,128)S(1)}, f32[16,6144]{1,0:T(8,128)S(1)}, u32[]{:S(2)}, u32[]{:S(2)}) %collective-permute-start.17) | collective-permute-done | bytes 393248 | tf_op jit(solution)/shard_map/ppermute | solution.py:212
  253.1 5.0 %collective-permute-done.19 = f32[128,6144]{1,0:T(8,128)S(1)} collective-permute-done((f32[128,6144]{1,0:T(8,128)S(1)}, f32[128,6144]{1,0:T(8,128)S(1)}, u32[]{:S(2)}, u32[]{:S(2)}) %collective-permute-start.19) | collective-permute-done | bytes 3145760 | tf_op jit(solution)/shard_map/ppermute | solution.py:212
  258.6 2.7 %copy-done.1 = f32[256,6144]{1,0:T(8,128)} copy-done((f32[256,6144]{1,0:T(8,128)}, f32[256,6144]{1,0:T(8,128)S(1)}, u32[]{:S(2)}) %copy-start.1) | copy-done | bytes 6291480
  (119 shorter events, 60.6 us)
Async XLA Ops:
  0.6 60.8 %copy-start = (f32[64,48]{0,1:T(8,128)S(1)}, f32[64,48]{0,1:T(8,128)}, u32[]{:S(2)}) copy-start(f32[64,48]{0,1:T(8,128)} %param.11) | copy-start | bytes 36868
  0.7 20.8 %collective-permute-start = (f32[32,6144]{1,0:T(8,128)}, f32[32,6144]{1,0:T(8,128)S(1)}, u32[]{:S(2)}, u32[]{:S(2)}) collective-permute-start(f32[32,6144]{1,0:T(8,128)} %param.8), channel_id=1, source_target_pairs={{0,8},{4,12},{8,0},{12,4},{16,24},{20,28},{24,16},{28,20},{1,9},{5... | collective-permute-start | bytes 2359304 | tf_op jit(solution)/shard_map/ppermute | solution.py:212
  3.7 19.6 %collective-permute-start.1 = (f32[32,6144]{1,0:T(8,128)}, f32[32,6144]{1,0:T(8,128)S(1)}, u32[]{:S(2)}, u32[]{:S(2)}) collective-permute-start(f32[32,6144]{1,0:T(8,128)} %param.8), channel_id=1, source_target_pairs={{0,16},{4,20},{8,24},{12,28},{16,0},{20,4},{24,8},{28,12},{1,17},{... | collective-permute-start | bytes 2359304 | tf_op jit(solution)/shard_map/ppermute | solution.py:212
  9.9 31.1 %copy-start.10 = (f32[48]{0:T(128)S(1)}, f32[48]{0:T(128)}, u32[]{:S(2)}) copy-start(f32[48]{0:T(128)} %param.12) | copy-start | bytes 580
  9.9 31.8 %copy-start.12 = (u32[32]{0:T(128)S(1)}, u32[32]{0:T(128)}, u32[]{:S(2)}) copy-start(u32[32]{0:T(128)} %constant.51) | copy-start | bytes 388
  21.4 10.4 %collective-permute-start.2 = (f32[16,6144]{1,0:T(8,128)S(1)}, f32[16,6144]{1,0:T(8,128)S(1)}, u32[]{:S(2)}, u32[]{:S(2)}) collective-permute-start(f32[16,6144]{1,0:T(8,128)S(1)} %slice.168), channel_id=1, source_target_pairs={{0,16},{4,20},{8,24},{12,28},{16,0},{20,4},{24,8},{28,12},{1,17},{... | collective-permute-start | bytes 1179656 | tf_op jit(solution)/shard_map/ppermute | solution.py:212
  23.3 9.8 %collective-permute-start.3 = (f32[16,6144]{1,0:T(8,128)S(1)}, f32[16,6144]{1,0:T(8,128)S(1)}, u32[]{:S(2)}, u32[]{:S(2)}) collective-permute-start(f32[16,6144]{1,0:T(8,128)S(1)} %slice.169), channel_id=1, source_target_pairs={{0,8},{4,12},{8,0},{12,4},{16,24},{20,28},{24,16},{28,20},{1,9},{5... | collective-permute-start | bytes 1179656 | tf_op jit(solution)/shard_map/ppermute | solution.py:212
  33.9 31.1 %collective-permute-start.4 = (f32[128,6144]{1,0:T(8,128)}, f32[128,6144]{1,0:T(8,128)}, u32[]{:S(2)}, u32[]{:S(2)}) collective-permute-start(f32[128,6144]{1,0:T(8,128)} %constant_dynamic-update-slice_fusion), channel_id=1, source_target_pairs={{0,4},{4,0},{8,12},{12,8},{16,20},{20,16},{24,28},{28,24},{1,5},{5... | collective-permute-start | bytes 9437192 | tf_op jit(solution)/shard_map/ppermute | solution.py:212
  77.3 58.2 %copy-start.9 = (f32[48]{0:T(128)S(1)}, f32[48]{0:T(128)}, u32[]{:S(2)}) copy-start(f32[48]{0:T(128)} %param.13) | copy-start | bytes 580
  119.7 1.4 collective-permute-start.5
  121.8 3.7 %collective-permute-start.6 = (f32[2,256]{1,0:T(2,128)S(1)}, f32[2,256]{1,0:T(2,128)S(1)}, u32[]{:S(2)}, u32[]{:S(2)}) collective-permute-start(f32[2,256]{1,0:T(2,128)S(1)} %pad_maximum_fusion.1), channel_id=1, source_target_pairs={{0,8},{4,12},{8,0},{12,4},{16,24},{20,28},{24,16},{28,20},{1,9},{5... | collective-permute-start | bytes 6152 | tf_op jit(solution)/shard_map/ppermute | solution.py:212
  125.5 3.7 %collective-permute-start.7 = (f32[2,256]{1,0:T(2,128)S(1)}, f32[2,256]{1,0:T(2,128)S(1)}, u32[]{:S(2)}, u32[]{:S(2)}) collective-permute-start(f32[2,256]{1,0:T(2,128)S(1)} %pad_maximum_fusion.2), channel_id=1, source_target_pairs={{0,16},{4,20},{8,24},{12,28},{16,0},{20,4},{24,8},{28,12},{1,17},{... | collective-permute-start | bytes 6152 | tf_op jit(solution)/shard_map/ppermute | solution.py:212
  129.2 3.7 %collective-permute-start.8 = (f32[2,256]{1,0:T(2,128)S(1)}, f32[2,256]{1,0:T(2,128)S(1)}, u32[]{:S(2)}, u32[]{:S(2)}) collective-permute-start(f32[2,256]{1,0:T(2,128)S(1)} %pad_maximum_fusion.3), channel_id=1, source_target_pairs={{0,1},{1,0},{2,3},{3,2},{4,5},{5,4},{6,7},{7,6},{8,9},{9,8},{10,11... | collective-permute-start | bytes 6152 | tf_op jit(solution)/shard_map/ppermute | solution.py:212
  132.8 4.5 %collective-permute-start.9 = (f32[2,256]{1,0:T(2,128)S(1)}, f32[2,256]{1,0:T(2,128)S(1)}, u32[]{:S(2)}, u32[]{:S(2)}) collective-permute-start(f32[2,256]{1,0:T(2,128)S(1)} %pad_maximum_fusion.4), channel_id=1, source_target_pairs={{0,2},{1,3},{2,0},{3,1},{4,6},{5,7},{6,4},{7,5},{8,10},{9,11},{10,... | collective-permute-start | bytes 6152 | tf_op jit(solution)/shard_map/ppermute | solution.py:212
  192.4 1.4 collective-permute-start.10
  194.5 3.7 %collective-permute-start.11 = (f32[2,256]{1,0:T(2,128)S(1)}, f32[2,256]{1,0:T(2,128)S(1)}, u32[]{:S(2)}, u32[]{:S(2)}) collective-permute-start(f32[2,256]{1,0:T(2,128)S(1)} %pad_maximum_fusion.6), channel_id=1, source_target_pairs={{0,8},{4,12},{8,0},{12,4},{16,24},{20,28},{24,16},{28,20},{1,9},{5... | collective-permute-start | bytes 6152 | tf_op jit(solution)/shard_map/ppermute | solution.py:212
  198.2 3.7 %collective-permute-start.12 = (f32[2,256]{1,0:T(2,128)S(1)}, f32[2,256]{1,0:T(2,128)S(1)}, u32[]{:S(2)}, u32[]{:S(2)}) collective-permute-start(f32[2,256]{1,0:T(2,128)S(1)} %pad_maximum_fusion.7), channel_id=1, source_target_pairs={{0,16},{4,20},{8,24},{12,28},{16,0},{20,4},{24,8},{28,12},{1,17},{... | collective-permute-start | bytes 6152 | tf_op jit(solution)/shard_map/ppermute | solution.py:212
  201.9 3.7 %collective-permute-start.13 = (f32[2,256]{1,0:T(2,128)S(1)}, f32[2,256]{1,0:T(2,128)S(1)}, u32[]{:S(2)}, u32[]{:S(2)}) collective-permute-start(f32[2,256]{1,0:T(2,128)S(1)} %pad_maximum_fusion.8), channel_id=1, source_target_pairs={{0,1},{1,0},{2,3},{3,2},{4,5},{5,4},{6,7},{7,6},{8,9},{9,8},{10,11... | collective-permute-start | bytes 6152 | tf_op jit(solution)/shard_map/ppermute | solution.py:212
  205.6 4.5 %collective-permute-start.14 = (f32[2,256]{1,0:T(2,128)S(1)}, f32[2,256]{1,0:T(2,128)S(1)}, u32[]{:S(2)}, u32[]{:S(2)}) collective-permute-start(f32[2,256]{1,0:T(2,128)S(1)} %pad_maximum_fusion.9), channel_id=1, source_target_pairs={{0,2},{1,3},{2,0},{3,1},{4,6},{5,7},{6,4},{7,5},{8,10},{9,11},{10,... | collective-permute-start | bytes 6152 | tf_op jit(solution)/shard_map/ppermute | solution.py:212
  225.8 16.9 %collective-permute-start.15 = (f32[32,6144]{1,0:T(8,128)}, f32[32,6144]{1,0:T(8,128)S(1)}, u32[]{:S(2)}, u32[]{:S(2)}) collective-permute-start(f32[32,6144]{1,0:T(8,128)} %update.3), channel_id=1, source_target_pairs={{0,8},{4,12},{8,0},{12,4},{16,24},{20,28},{24,16},{28,20},{1,9},{5... | collective-permute-start | bytes 2359304 | tf_op jit(solution)/shard_map/ppermute | solution.py:212
  225.8 18.2 %collective-permute-start.16 = (f32[32,6144]{1,0:T(8,128)}, f32[32,6144]{1,0:T(8,128)S(1)}, u32[]{:S(2)}, u32[]{:S(2)}) collective-permute-start(f32[32,6144]{1,0:T(8,128)} %update.3), channel_id=1, source_target_pairs={{0,16},{4,20},{8,24},{12,28},{16,0},{20,4},{24,8},{28,12},{1,17},{... | collective-permute-start | bytes 2359304 | tf_op jit(solution)/shard_map/ppermute | solution.py:212
  242.8 7.8 %collective-permute-start.17 = (f32[16,6144]{1,0:T(8,128)S(1)}, f32[16,6144]{1,0:T(8,128)S(1)}, u32[]{:S(2)}, u32[]{:S(2)}) collective-permute-start(f32[16,6144]{1,0:T(8,128)S(1)} %slice.194), channel_id=1, source_target_pairs={{0,16},{4,20},{8,24},{12,28},{16,0},{20,4},{24,8},{28,12},{1,17},{... | collective-permute-start | bytes 1179656 | tf_op jit(solution)/shard_map/ppermute | solution.py:212
  244.1 8.3 %collective-permute-start.18 = (f32[16,6144]{1,0:T(8,128)S(1)}, f32[16,6144]{1,0:T(8,128)S(1)}, u32[]{:S(2)}, u32[]{:S(2)}) collective-permute-start(f32[16,6144]{1,0:T(8,128)S(1)} %slice.195), channel_id=1, source_target_pairs={{0,8},{4,12},{8,0},{12,4},{16,24},{20,28},{24,16},{28,20},{1,9},{5... | collective-permute-start | bytes 1179656 | tf_op jit(solution)/shard_map/ppermute | solution.py:212
  252.4 5.7 %collective-permute-start.19 = (f32[128,6144]{1,0:T(8,128)S(1)}, f32[128,6144]{1,0:T(8,128)S(1)}, u32[]{:S(2)}, u32[]{:S(2)}) collective-permute-start(f32[128,6144]{1,0:T(8,128)S(1)} %constant_dynamic-update-slice_fusion.5), channel_id=1, source_target_pairs={{0,4},{4,0},{8,12},{12,8},{16,20},{20,16},{24,28},{28,24},{1,5},{5... | collective-permute-start | bytes 9437192 | tf_op jit(solution)/shard_map/ppermute | solution.py:212
  (9 other events, 103.4 us)
